TPU v7x, 512 devices: a whole 4x8x8 slice. The times are simulated.
512 devices in a mesh: dp: 128 (over x, y_lo, z), pair: 4 (over y_hi, core).
Axes of the slice: x: 4, y: 8 (y_hi: 2, y_lo: 4; y = y_hi * 4 + y_lo), z: 8, core: 2. Of those that a mesh axis runs over, the one named last changes fastest.
Arguments:
- image_emb: bfloat16 [65536, 1152], P(('dp', 'pair')), may hold values from -0.19921875 to 0.19921875
- text_emb: bfloat16 [65536, 1152], P(('dp', 'pair')), may hold values from -0.19921875 to 0.19921875
- head_weight: bfloat16 [1152, 1152], replicated, may hold values from -0.1875 to 0.1875
- natural_exponent_multiplier: float32 [1], replicated, may hold values from 1.5 to 2.5
- bias: float32 [1], replicated, may hold values from -7 to -4
Outputs:
- loss: float32 [65536], P(('dp', 'pair'))
- image_grad: float32 [65536, 1152], P(('dp', 'pair'))
- text_grad: float32 [65536, 1152], P(('dp', 'pair'))
- head_grad: float32 [1152, 1152], P('dp', 'pair')
All inputs are finite; a program needn't handle non-finite values.
Results may differ from a plain program's by a relative error of at most 0.0051.
Values may be sent and summed in bfloat16 or wider, within the bound.
A program may use at most 64 MiB of HBM per device.

v0:
```python
import jax
import jax.numpy as jnp
from jax import lax
from jax.sharding import PartitionSpec as P

WINDOW = 3


epsilon = 1e-06


def shifted(value, axis, steps):
    count = lax.axis_size(axis)
    pairs = [(source, (source + steps) % count) for source in range(count)]
    return lax.ppermute(value, axis, pairs)


def sample_subrange_length(left, right):
    return lax.dot_general(
        left, right, (((1,), (1,)), ((), ())), preferred_element_type=jnp.float32
    )


def inner_cols(left, right):
    return lax.dot_general(
        left, right, (((0,), (0,)), ((), ())), preferred_element_type=jnp.float32
    )


def body(image_emb, text_emb, head_weight, natural_exponent_multiplier, bias):
    row_count, feat_width = image_emb.shape
    pair_count = lax.axis_size("pair")
    pair_index = lax.axis_index("pair")
    similarity_sharpness_factor = jnp.exp(natural_exponent_multiplier[0])
    similarity_additive_shift = bias[0]
    projected = jnp.dot(image_emb, head_weight, preferred_element_type=jnp.float32)
    image_scale = lax.rsqrt(jnp.sum(projected * projected, axis=1, keepdims=True) + epsilon)
    image_unit = projected * image_scale
    picture_embedding_matrix = image_unit.astype(jnp.bfloat16)
    text_wide = text_emb.astype(jnp.float32)
    text_scale = lax.rsqrt(jnp.sum(text_wide * text_wide, axis=1, keepdims=True) + epsilon)
    text_unit = text_wide * text_scale
    text_feat = text_unit.astype(jnp.bfloat16)
    group_rows = row_count * pair_count
    own_mask = (
        jnp.arange(group_rows, dtype=jnp.int32)[None, :]
        == (pair_index * row_count + jnp.arange(row_count, dtype=jnp.int32))[:, None]
    ).astype(jnp.float32)
    arriving_picture_piece = [lax.all_gather(text_feat, "pair", axis=0, tiled=True)]
    for rotation_shift_amount in range(1, WINDOW):
        arriving_picture_piece.append(shifted(arriving_picture_piece[-1], "dp", 1))
    loss_rows = jnp.zeros((row_count,), jnp.float32)
    image_dir = jnp.zeros((row_count, feat_width), jnp.float32)
    text_parts = []
    for rotation_shift_amount in range(WINDOW):
        similarity_matrix_entries = (
            similarity_sharpness_factor
            * sample_subrange_length(
                picture_embedding_matrix, arriving_picture_piece[rotation_shift_amount]
            )
            + similarity_additive_shift
        )
        matching_target_sign = own_mask * (1.0 if rotation_shift_amount == 0 else 0.0)
        loss_rows = loss_rows + jnp.sum(
            jax.nn.softplus(similarity_matrix_entries)
            - matching_target_sign * similarity_matrix_entries,
            axis=1,
        )
        objective_weighting_factor = (
            similarity_sharpness_factor
            * (jax.nn.sigmoid(similarity_matrix_entries) - matching_target_sign)
        ).astype(jnp.bfloat16)
        image_dir = image_dir + jnp.dot(
            objective_weighting_factor,
            arriving_picture_piece[rotation_shift_amount],
            preferred_element_type=jnp.float32,
        )
        text_parts.append(inner_cols(objective_weighting_factor, picture_embedding_matrix))
    carried = text_parts[0]
    for rotation_shift_amount in range(1, WINDOW):
        carried = shifted(carried, "dp", 1) + text_parts[rotation_shift_amount]
    carried = shifted(carried, "dp", -(WINDOW - 1))
    text_dir = lax.psum_scatter(carried, "pair", scatter_dimension=0, tiled=True)
    along = jnp.sum(image_unit * image_dir, axis=1, keepdims=True)
    pre_grad = (image_scale * (image_dir - image_unit * along)).astype(jnp.bfloat16)
    image_grad = sample_subrange_length(pre_grad, head_weight)
    col_count = feat_width // pair_count
    rows_piece = lax.all_gather(image_emb, "pair", axis=0, tiled=True)
    grad_piece = lax.all_gather(pre_grad, "pair", axis=0, tiled=True)
    grad_cols = lax.dynamic_slice_in_dim(grad_piece, pair_index * col_count, col_count, 1)
    partial_head = inner_cols(rows_piece, grad_cols)
    head_grad = lax.psum_scatter(partial_head, "dp", scatter_dimension=0, tiled=True)
    text_along = jnp.sum(text_unit * text_dir, axis=1, keepdims=True)
    text_grad = text_scale * (text_dir - text_unit * text_along)
    return (loss_rows, image_grad, text_grad, head_grad)


def solution(mesh):
    return jax.shard_map(
        body,
        mesh=mesh,
        in_specs=(P(("dp", "pair"), None), P(("dp", "pair"), None), P(), P(), P()),
        out_specs=(
            P(("dp", "pair")),
            P(("dp", "pair"), None),
            P(("dp", "pair"), None),
            P("dp", "pair"),
        ),
        check_vma=False,
    )
```

profile of v0, /device:TPU:56, one launch (start us, length us, event | category | flops | bytes accessed | tf_op | source)
XLA Modules:
  0.0 1708.5 jit_solution(10944629152296829720)
XLA Ops:
  8.5 1.8 fusion.5
  12.6 33.5 %all-gather.4.cloned.1.call-done = bf16[512,1152]{1,0:T(8,128)(2,1)} async-done(((bf16[128,1152]{1,0:T(8,128)(2,1)}), bf16[512,1152]{1,0:T(8,128)(2,1)}) %all-gather.4.cloned.1.call-update) | async-done | bytes 1179664 | tf_op jit(solution)/shard_map/all_gather | solution.py:49
  46.0 2.0 fusion.12
  48.1 2.0 fusion.19
  50.1 3.6 collective-permute-start.2
  53.6 3.5 collective-permute-start
  57.3 90.7 %collective-permute-done = bf16[512,1152]{1,0:T(8,128)(2,1)} collective-permute-done((bf16[512,1152]{1,0:T(8,128)(2,1)}, bf16[512,1152]{1,0:T(8,128)(2,1)}, u32[]{:S(2)}, u32[]{:S(2)}) %collective-permute-start) | collective-permute-done | bytes 1179680 | tf_op jit(solution)/shard_map/ppermute | solution.py:15
  147.9 1.9 collective-permute-start.1
  149.9 1.8 fusion.20
  151.6 2.0 fusion.14
  153.6 3.6 convolution_add_fusion
  157.2 1.9 collective-permute-start.3
  159.2 1.6 convolution_add_fusion.2
  160.8 20.2 %collective-permute-done.1 = bf16[512,1152]{1,0:T(8,128)(2,1)S(1)} collective-permute-done((bf16[512,1152]{1,0:T(8,128)(2,1)}, bf16[512,1152]{1,0:T(8,128)(2,1)S(1)}, u32[]{:S(2)}, u32[]{:S(2)}) %collective-permute-start.1) | collective-permute-done | bytes 1179680 | tf_op jit(solution)/shard_map/ppermute | solution.py:15
  184.0 1.5 fusion.18
  185.5 57.6 %collective-permute-done.3 = f32[512,1152]{1,0:T(8,128)} collective-permute-done((f32[512,1152]{1,0:T(8,128)}, f32[512,1152]{1,0:T(8,128)}, u32[]{:S(2)}, u32[]{:S(2)}) %collective-permute-start.3) | collective-permute-done | bytes 2359328 | tf_op jit(solution)/shard_map/ppermute | solution.py:15
  243.1 3.4 add.103
  246.5 1.9 collective-permute-start.4
  248.4 3.3 convolution_bitcast_fusion
  251.8 98.1 %collective-permute-done.4 = f32[512,1152]{1,0:T(8,128)} collective-permute-done((f32[512,1152]{1,0:T(8,128)}, f32[512,1152]{1,0:T(8,128)}, u32[]{:S(2)}, u32[]{:S(2)}) %collective-permute-start.4) | collective-permute-done | bytes 2359328 | tf_op jit(solution)/shard_map/ppermute | solution.py:15
  352.4 1.7 fusion.21
  354.1 1256.8 %all-reduce.3.cloned.1.call-done = f32[1152,288]{0,1:T(8,128)} async-done(((f32[1152,288]{0,1:T(8,128)}), f32[1152,288]{0,1:T(8,128)}) %all-reduce.3.cloned.1.call-update) | async-done | bytes 1327120
  1612.7 86.9 %reduce-scatter.3.cloned.1.call-done = f32[128,1152]{1,0:T(8,128)} async-done(((f32[512,1152]{1,0:T(8,128)}), f32[128,1152]{1,0:T(8,128)}) %reduce-scatter.3.cloned.1.call-update) | async-done | bytes 589840 | tf_op jit(solution)/shard_map/reduce_scatter | solution.py:83
  1699.6 1.4 fusion.6
  (43 shorter events, 10.0 us)
Async XLA Ops:
  7.2 4.6 copy-start
  7.2 4.6 copy-start.4
  7.2 38.9 %all-gather.4.cloned.1.call-start = ((), (), s32[]{:S(2)}) async-start(), calls=%async_computation.1 | async-start | bytes 1474560 | tf_op jit(solution)/shard_map/all_gather | solution.py:49
  10.3 238.1 %all-gather.8.cloned.1.call-start = ((), (), s32[]{:S(2)}) async-start(), calls=%async_computation.4 | async-start | bytes 1474560 | tf_op jit(solution)/shard_map/all_gather | solution.py:88
  48.1 2.0 copy-start.6
  50.1 103.6 %collective-permute-start.2 = (f32[512,1152]{1,0:T(8,128)}, f32[512,1152]{1,0:T(8,128)}, u32[]{:S(2)}, u32[]{:S(2)}) collective-permute-start(f32[512,1152]{1,0:T(8,128)} %fusion.19), channel_id=1, source_target_pairs={{0,4},{4,8},{8,12},{12,16},{16,20},{20,24},{24,28},{28,32},{32,36}... | collective-permute-start | bytes 7077896 | tf_op jit(solution)/shard_map/ppermute | solution.py:15
  53.6 94.3 %collective-permute-start = (bf16[512,1152]{1,0:T(8,128)(2,1)}, bf16[512,1152]{1,0:T(8,128)(2,1)}, u32[]{:S(2)}, u32[]{:S(2)}) collective-permute-start(bf16[512,1152]{1,0:T(8,128)(2,1)} %all-gather.4.cloned.1.call-done), channel_id=1, source_target_pairs={{0,4},{4,8},{8,12},{12,16},{16,20},{20,24},{24,28},{28,32},{32,36}... | collective-permute-start | bytes 3538952 | tf_op jit(solution)/shard_map/ppermute | solution.py:15
  57.2 191.2 %all-gather.6.cloned.1.call-start = ((), (), s32[]{:S(2)}) async-start(), calls=%async_computation.3 | async-start | bytes 1474560 | tf_op jit(solution)/shard_map/all_gather | solution.py:89
  147.9 33.1 %collective-permute-start.1 = (bf16[512,1152]{1,0:T(8,128)(2,1)}, bf16[512,1152]{1,0:T(8,128)(2,1)S(1)}, u32[]{:S(2)}, u32[]{:S(2)}) collective-permute-start(bf16[512,1152]{1,0:T(8,128)(2,1)} %collective-permute-done), channel_id=1, source_target_pairs={{0,4},{4,8},{8,12},{12,16},{16,20},{20,24},{24,28},{28,32},{32,36}... | collective-permute-start | bytes 3538952 | tf_op jit(solution)/shard_map/ppermute | solution.py:15
  157.2 85.8 %collective-permute-start.3 = (f32[512,1152]{1,0:T(8,128)}, f32[512,1152]{1,0:T(8,128)}, u32[]{:S(2)}, u32[]{:S(2)}) collective-permute-start(f32[512,1152]{1,0:T(8,128)} %convolution_add_fusion), channel_id=1, source_target_pairs={{0,4},{4,8},{8,12},{12,16},{16,20},{20,24},{24,28},{28,32},{32,36}... | collective-permute-start | bytes 7077896 | tf_op jit(solution)/shard_map/ppermute | solution.py:15
  182.3 0.7 copy-start.5
  183.9 1427.0 %all-reduce.3.cloned.1.call-start = ((), (), s32[]{:S(2)}) async-start(), calls=%async_computation.5 | async-start | bytes 2654208
  246.5 103.4 %collective-permute-start.4 = (f32[512,1152]{1,0:T(8,128)}, f32[512,1152]{1,0:T(8,128)}, u32[]{:S(2)}, u32[]{:S(2)}) collective-permute-start(f32[512,1152]{1,0:T(8,128)} %add.103), channel_id=1, source_target_pairs={{0,504},{4,508},{8,0},{12,4},{16,8},{20,12},{24,16},{28,20},{32,24... | collective-permute-start | bytes 7077896 | tf_op jit(solution)/shard_map/ppermute | solution.py:15
  251.7 1447.8 %reduce-scatter.3.cloned.1.call-start = ((), (), s32[]{:S(2)}) async-start(), calls=%async_computation.2 | async-start | bytes 2949120 | tf_op jit(solution)/shard_map/reduce_scatter | solution.py:83
  349.9 2.0 copy-start.7
  349.9 2.5 copy-start.2
  352.4 1347.2 %copy-start.1 = (bf16[128,1152]{1,0:T(8,128)(2,1)S(1)}, bf16[128,1152]{1,0:T(8,128)(2,1)}, u32[]{:S(2)}) copy-start(bf16[128,1152]{1,0:T(8,128)(2,1)} %param.6) | copy-start | bytes 884740
  1699.6 1.4 copy-start.3
Sparse Core Ops, SparseCore 0:
  10.7 35.2 all-gather.3
  57.3 30.3 all-gather.7
  184.1 29.3 all-gather.5
  251.9 1359.0 all-reduce.2
  1614.1 85.3 reduce-scatter.2
where the time goes:
time: 1720 us; the launch traced here: 1710 us
  waiting for transfers between devices  1640 us (95%)
  matrix products  21.9 us (1%)
    unnamed x6, waiting for transfers between devices  1260 us
    ppermute x5, waiting for transfers between devices, shifted(): return lax.ppermute(value, axis, pairs)  267 us
    reduce_scatter x1, waiting for transfers between devices, body(): lax.psum_scatter(carried, 'pair', scatter_dimension=0, tiled=True)  86.9 us
  transfers between devices with their start and end apart: 10, of which 7 were waited for; matrix products, arithmetic and copies ran while one was open for 2% of the time, Pallas kernels for 0%

commit v1 on v0

v1 whole, which is shorter than its diff:
```python
import functools

import jax
import jax.numpy as jnp
import numpy as np
from jax import lax
from jax.experimental import pallas as pl
from jax.experimental.pallas import tpu as pltpu
from jax.sharding import PartitionSpec as P

NX, NYL, NZ = 4, 4, 8
NY = 2 * NYL
WINDOW = 3
ROWS = 128
BLOCK = 2 * ROWS
D = 1152
COLS = D // 4
PIECE = 80
HALF = 8 * PIECE
EPS = 1e-06
BF = jnp.bfloat16
F32 = jnp.float32

R_RAW, R_SIB, R_LOSS, R_EMB, R_PRE, R_ONE, R_FIN, R_ALL = 12, 13, 14, 15, 18, 21, 35, 43
S_K, S_RAW, S_Q, S_SIB, S_LOSS, S_EMB, S_PRE, S_ONE, S_FIN, S_ALL = 0, 10, 11, 12, 13, 14, 17, 20, 34, 50


def nt(left, right):
    return lax.dot_general(left, right, (((1,), (1,)), ((), ())), preferred_element_type=F32)


def nn(left, right):
    return jnp.dot(left, right, preferred_element_type=F32)


def select_matrix():
    row = np.arange(2 * HALF)
    half, piece, k = row // HALF, (row % HALF) // PIECE, row % PIECE
    block, inner = k // 9, k % 9
    source = np.where(half == 0, 72 * piece + k, 576 + 72 * block + 9 * piece + inner)
    return ((source[:, None] == np.arange(D)[None, :]) & (k < 72)[:, None]).astype(np.float32)


def kernel(
    nem, bias, img, txt, w_any, sel_any,
    loss_o, ig_o, tg_o, hg_o,
    w, sel, kbuf, raw, qf, unit, acc, pre, pre_t, sib_f32, sib_bf, loss_s, loss_r,
    emb_t, p_t, p_out, one, fin_s, fin_r, ssem, rsem, lsem,
):
    dp = lax.axis_index("dp")
    pair = lax.axis_index("pair")
    core = lax.rem(pair, 2)
    yh = lax.div(pair, 2)
    x = lax.div(dp, NYL * NZ)
    yl = lax.rem(lax.div(dp, NZ), NYL)
    z = lax.rem(dp, NZ)
    y = yh * NYL + yl

    def chip(cx, cy, cz, cc):
        return (cx * (NYL * NZ) + lax.rem(cy, NYL) * NZ + cz, lax.div(cy, NYL) * 2 + cc)

    sibling = (dp, yh * 2 + 1 - core)
    across = (dp, (1 - yh) * 2 + core)
    flip_to = jnp.where(lax.rem(dp, 32) == 31 * (1 - core), 1, 0)
    flip_from = jnp.where(lax.rem(dp, 32) == 31 * core, 1, 0)
    chain_to = (lax.rem(dp + 1 + 126 * core, 128), lax.rem(yh + flip_to, 2) * 2 + core)
    chain_from = (lax.rem(dp + 127 - 126 * core, 128), lax.rem(yh + flip_from, 2) * 2 + core)

    def x_dev(d):
        return chip(lax.rem(x + d, NX), y, z, core)

    def one_dev(h, d):
        if h == 0:
            return chip(x, lax.rem(y + d, NY), z, core)
        return chip(x, y, lax.rem(z + d, NZ), core)

    def fin_block(h, d):
        return lax.rem(z + d, 8) if h == 0 else lax.rem(y + d, 8)

    def fin_dev(h, d):
        block = fin_block(h, d)
        return (8 * y + block if h == 0 else 64 + 8 * block + z, x)

    low = jnp.where(dp < 64, 1, 0)
    q8 = lax.rem(lax.div(dp, 8), 8)

    def fin_from(d):
        ys = jnp.where(low == 1, q8, lax.rem(q8 + 8 - d, 8))
        zs = jnp.where(low == 1, lax.rem(z + 8 - d, 8), z)
        return chip(pair, ys, zs, 0)

    def is_me(device):
        return jnp.logical_and(device[0] == dp, device[1] == pair)

    barrier = pltpu.get_barrier_semaphore()

    def hello(device):
        pl.semaphore_signal(barrier, inc=1, device_id=device, device_id_type=pl.DeviceIdType.MESH)

    def copy(src, dst, send, recv, device):
        return pltpu.make_async_remote_copy(
            src_ref=src, dst_ref=dst, send_sem=ssem.at[send], recv_sem=rsem.at[recv],
            device_id=device, device_id_type=pl.DeviceIdType.MESH,
        )

    def normal(value):
        scale = lax.rsqrt(jnp.sum(value * value, axis=1, keepdims=True) + EPS)
        return value * scale, scale

    def run(role):
        own, oth = role, 1 - role
        own_rows = pl.ds(own * ROWS, ROWS)
        oth_rows = pl.ds(oth * ROWS, ROWS)
        w_copy = pltpu.make_async_copy(w_any, w, lsem.at[0])
        w_copy.start()
        hello(sibling)
        hello(across)
        hello(chain_from)
        if role == 0:
            sel_copy = pltpu.make_async_copy(sel_any, sel, lsem.at[1])
            sel_copy.start()
            for d in range(1, NX):
                hello(x_dev(NX - d))
            for h in range(2):
                for d in range(1, 8):
                    hello(one_dev(h, 8 - d))
        for d in range(8):
            device = fin_from(d)
            pl.when(jnp.logical_not(is_me(device)))(lambda device=device: hello(device))

        started = []

        def go(*args):
            c = copy(*args)
            c.start()
            started.append(c)

        def kslot(t, h, s):
            return kbuf.at[t, h, pl.ds(s * ROWS, ROWS)]

        def arrived(dst, recv):
            copy(dst, dst, 0, recv, sibling).wait_recv()

        def spread(s, send):
            go(kslot(0, 0, s), kslot(1, 0, s), send, 4 + s, chain_to)
            go(kslot(0, 0, s), kslot(0, 1, s), send + 1, 2 + s, across)

        t_unit, t_scale = normal(txt[...].astype(F32))
        if role == 0:
            kbuf[0, 0, own_rows] = t_unit.astype(BF)
            away = 3 + 3 + 14 + 16
            for h in range(2):
                for d in range(8):
                    away = away - jnp.where(is_me(fin_dev(h, d)), 1, 0)
            pl.semaphore_wait(barrier, away)
            spread(own, S_K)
            go(txt, raw.at[own_rows], S_RAW, R_RAW, sibling)
            w_copy.wait()
            i_unit, i_scale = normal(nn(img[...], w[...]))
            unit[own_rows] = i_unit
            qf[own_rows] = i_unit.astype(BF)
            go(qf.at[own_rows], kslot(0, 0, own), S_Q, own, sibling)
            raw[own_rows] = img[...]
        else:
            unit[own_rows] = t_unit
            qf[own_rows] = t_unit.astype(BF)
            pl.semaphore_wait(barrier, 3)
            go(qf.at[own_rows], kslot(0, 0, own), S_Q, own, sibling)
            go(img, raw.at[own_rows], S_RAW, R_RAW, sibling)
            w_copy.wait()
            i_unit, i_scale = normal(nn(img[...], w[...]))
            kbuf[0, 0, own_rows] = i_unit.astype(BF)
            spread(own, S_K)
            raw[own_rows] = txt[...]
        own_scale = i_scale if role == 0 else t_scale
        arrived(kslot(0, 0, oth), oth)
        spread(oth, S_K + 2)
        arrived(raw.at[oth_rows], R_RAW)
        if role == 0:
            o_unit, oth_scale = normal(nn(raw[oth_rows], w[...]))
        else:
            o_unit, oth_scale = normal(raw[oth_rows].astype(F32))
        unit[oth_rows] = o_unit
        qf[oth_rows] = o_unit.astype(BF)

        gain = jnp.exp(jnp.full((1, 1), nem[0], F32))
        shift = bias[0]
        if role == 0:
            sel_copy.wait()
            for part in range(4):
                rows = pl.ds(part * (HALF // 2), HALF // 2)
                emb_t[0, rows] = nt(sel[rows], raw[...]).astype(BF)
            for d in range(1, NX):
                go(emb_t.at[0], emb_t.at[d], S_EMB + d - 1, R_EMB + d - 1, x_dev(d))

        loss = jnp.zeros((BLOCK, 1), F32)

        def score(t, h, loss):
            k = kbuf[t, h]
            s = gain * nt(qf[...], k) + shift
            e = jnp.exp(-jnp.abs(s))
            sig = jnp.where(s >= 0, 1.0, e) / (1.0 + e)
            label = None
            if t == 0 and h == 0:
                r = lax.broadcasted_iota(jnp.int32, (BLOCK, BLOCK), 0)
                c = lax.broadcasted_iota(jnp.int32, (BLOCK, BLOCK), 1)
                label = jnp.where(r == c, 1.0, 0.0)
                sig = sig - label
            if role == 0:
                term = jnp.maximum(s, 0.0) + jnp.log1p(e)
                if label is not None:
                    term = term - label * s
                loss = loss + jnp.sum(term, axis=1, keepdims=True)
            value = nn((gain * sig).astype(BF), k)
            if label is not None:
                acc[...] = value
            else:
                acc[...] += value
            return loss

        loss = score(0, 0, loss)
        send = S_K + 4
        for t, h in ((1, 0), (0, 1), (1, 1)):
            for s in (own, oth):
                arrived(kslot(t, h, s), 4 * t + 2 * h + s)
                go(kslot(t, h, s), kslot(t + 1, h, s), send, 4 * t + 4 + 2 * h + s, chain_to)
                send += 1
            loss = score(t, h, loss)
        for h in range(2):
            for s in (own, oth):
                arrived(kslot(2, h, s), 8 + 2 * h + s)
            loss = score(2, h, loss)

        for half_rows, scale in ((own_rows, own_scale), (oth_rows, oth_scale)):
            u = unit[half_rows]
            a = acc[half_rows]
            along = jnp.sum(u * a, axis=1, keepdims=True)
            g = scale * (a - u * along)
            if role == 0:
                pre[half_rows] = g.astype(BF)
                pre_t[:, half_rows] = jnp.transpose(g).astype(BF)
            elif half_rows is own_rows:
                tg_o[...] = g
            else:
                unit[half_rows] = g

        if role == 0:
            for d in range(1, NX):
                start = pl.multiple_of(lax.rem(x + d, NX) * COLS, 16)
                go(pre_t.at[pl.ds(start, COLS)], p_t.at[d], S_PRE + d - 1, R_PRE + d - 1, x_dev(d))
            go(pre.at[oth_rows], sib_bf, S_SIB, R_SIB, sibling)
            turned = jnp.transpose(jnp.broadcast_to(loss, (BLOCK, 128)))
            loss_o[...] = turned[0:1, 0:ROWS]
            loss_s[...] = turned[0:8, ROWS:BLOCK]
            go(loss_s, loss_r, S_LOSS, R_LOSS, sibling)
            start = pl.multiple_of(x * COLS, 16)
            p_t[0] = pre_t[pl.ds(start, COLS)]
            for d in range(1, NX):
                arrived(p_t.at[d], R_PRE + d - 1)
                arrived(emb_t.at[d], R_EMB + d - 1)

            def product(h, d):
                index = lax.rem((y if h == 0 else z) + d, 8)
                rows = pl.ds(pl.multiple_of(h * HALF + index * PIECE, 16), PIECE)
                total = nt(emb_t[0, rows], p_t[0])
                for k in range(1, NX):
                    total = total + nt(emb_t[k, rows], p_t[k])
                return total

            for d in (4, 3, 5, 2, 6, 1, 7):
                for h in range(2):
                    i = 7 * h + d - 1
                    p_out[i] = product(h, d).astype(BF)
                    go(p_out.at[i], one.at[i], S_ONE + i, R_ONE + i, one_dev(h, d))
            totals = [product(0, 0), product(1, 0)]
            ig_o[...] = nt(pre[own_rows], w[...])
            r = lax.broadcasted_iota(jnp.int32, (128, PIECE), 0)
            c = lax.broadcasted_iota(jnp.int32, (128, PIECE), 1)
            inner = jnp.bitwise_and(r, 15)
            pick = jnp.logical_and(inner < 9, c == 9 * jnp.right_shift(r, 4) + inner)
            pick = jnp.where(pick, 1.0, 0.0).astype(BF)
            for h in range(2):
                total = totals[h]
                for d in range(1, 8):
                    i = 7 * h + d - 1
                    arrived(one.at[i], R_ONE + i)
                    total = total + one[i].astype(F32)
                blocks = nn(pick, total.astype(BF)).astype(BF)
                for i in range(8):
                    fin_s[h, i] = blocks[16 * i : 16 * i + 16]
                for d in range(8):
                    device = fin_dev(h, d)
                    block = fin_block(h, d)
                    me = is_me(device)
                    c = copy(fin_s.at[h, block], fin_r.at[d], S_FIN + 8 * h + d, R_FIN + d, device)

                    @pl.when(me)
                    def _(d=d, block=block, h=h):
                        fin_r[d] = fin_s[h, block]

                    @pl.when(jnp.logical_not(me))
                    def _(c=c):
                        c.start()

            arrived(sib_f32, R_SIB)
            tg_o[...] = sib_f32[...]
        else:
            go(unit.at[oth_rows], sib_f32, S_SIB, R_SIB, sibling)
            arrived(sib_bf, R_SIB)
            ig_o[...] = nt(sib_bf[...], w[...])
            arrived(loss_r, R_LOSS)
            loss_o[...] = loss_r[0:1]

        for d in range(8):
            me = is_me(fin_from(d))

            @pl.when(jnp.logical_not(me))
            def _(d=d):
                arrived(fin_r.at[d], R_FIN + d)

        total = fin_r[0].astype(F32)
        for d in range(1, 8):
            total = total + fin_r[d].astype(F32)
        hg_o[...] = total[0:9]
        for c in started:
            c.wait_send()
        if role == 0:
            for h in range(2):
                for d in range(8):
                    device = fin_dev(h, d)
                    c = copy(
                        fin_s.at[h, fin_block(h, d)], fin_r.at[d], S_FIN + 8 * h + d, R_FIN + d, device
                    )
                    pl.when(jnp.logical_not(is_me(device)))(lambda c=c: c.wait_send())

    pl.when(core == 0)(lambda: run(0))
    pl.when(core == 1)(lambda: run(1))


def body(image_emb, text_emb, head_weight, natural_exponent_multiplier, bias):
    vmem = pl.BlockSpec(memory_space=pltpu.VMEM)
    smem = pl.BlockSpec(memory_space=pltpu.SMEM)
    hbm = pl.BlockSpec(memory_space=pl.ANY)
    loss, image_grad, text_grad, head_grad = pl.pallas_call(
        kernel,
        name="contrast",
        out_shape=(
            jax.ShapeDtypeStruct((1, ROWS), F32),
            jax.ShapeDtypeStruct((ROWS, D), F32),
            jax.ShapeDtypeStruct((ROWS, D), F32),
            jax.ShapeDtypeStruct((9, COLS), F32),
        ),
        in_specs=[smem, smem, vmem, vmem, hbm, hbm],
        out_specs=(vmem, vmem, vmem, vmem),
        scratch_shapes=[
            pltpu.VMEM((D, D), BF),
            pltpu.VMEM((2 * HALF, D), BF),
            pltpu.VMEM((WINDOW, 2, BLOCK, D), BF),
            pltpu.VMEM((BLOCK, D), BF),
            pltpu.VMEM((BLOCK, D), BF),
            pltpu.VMEM((BLOCK, D), F32),
            pltpu.VMEM((BLOCK, D), F32),
            pltpu.VMEM((BLOCK, D), BF),
            pltpu.VMEM((D, BLOCK), BF),
            pltpu.VMEM((ROWS, D), F32),
            pltpu.VMEM((ROWS, D), BF),
            pltpu.VMEM((8, ROWS), F32),
            pltpu.VMEM((8, ROWS), F32),
            pltpu.VMEM((NX, 2 * HALF, BLOCK), BF),
            pltpu.VMEM((NX, COLS, BLOCK), BF),
            pltpu.VMEM((14, PIECE, COLS), BF),
            pltpu.VMEM((14, PIECE, COLS), BF),
            pltpu.VMEM((2, 8, 16, COLS), BF),
            pltpu.VMEM((8, 16, COLS), BF),
            pltpu.SemaphoreType.DMA((S_ALL,)),
            pltpu.SemaphoreType.DMA((R_ALL,)),
            pltpu.SemaphoreType.DMA((2,)),
        ],
        compiler_params=pltpu.CompilerParams(
            collective_id=0, has_side_effects=True, vmem_limit_bytes=56 * 2**20
        ),
    )(
        natural_exponent_multiplier,
        bias,
        image_emb,
        text_emb,
        head_weight,
        jnp.asarray(select_matrix(), BF),
    )
    return loss.reshape(ROWS), image_grad, text_grad, head_grad


def solution(mesh):
    return jax.shard_map(
        body,
        mesh=mesh,
        in_specs=(P(("dp", "pair"), None), P(("dp", "pair"), None), P(), P(), P()),
        out_specs=(
            P(("dp", "pair")),
            P(("dp", "pair"), None),
            P(("dp", "pair"), None),
            P("dp", "pair"),
        ),
        check_vma=False,
    )
```

time: 1720 us -> 111 us (0.06)
  the two profiles are of different devices: /device:TPU:56 before, /device:TPU:12 now
where the time goes in v1:
time: 111 us; the launch traced here: 110 us
  Pallas kernels  102 us (92%)
  local copies, waits for them, and re-layouts  6.31 us (6%)
  between operations  1.93 us (2%)
    pallas_call x1, Pallas kernels, body(): pl.pallas_call(kernel, name='contrast', out_shape=(jax.ShapeDtypeStruct((...  102 us
    unnamed x4, local copies, waits for them, and re-layouts  6.31 us

profile of v1, /device:TPU:12, one launch (start us, length us, event | category | flops | bytes accessed | tf_op | source)
XLA Modules:
  0.0 110.2 jit_solution(4035883597647453669)
XLA Ops:
  1.9 102.0 %contrast.1 = (f32[1,128]{1,0:T(1,128)}, f32[128,1152]{1,0:T(8,128)}, f32[128,1152]{1,0:T(8,128)}, f32[9,288]{1,0:T(8,128)}) custom-call(f32[1]{0:T(128)S(6)} %copy.14.nem, f32[1]{0:T(128)S(6)} %copy.15.bias, bf16[128,1152]{1,0:T(8,128)(2,1)} %img.1, bf16[128,1152]{1,0:T(8,128)(2,1)} %txt.1, bf16[1152,1152]{1,0:T(8,128)(2,1)} %w_any.1, ...), custom_call_target="tpu_custom_call" | custom-call | tf_op jit(solution)/shard_map/contrast/pallas_call | solution.py:344
  103.9 1.1 %copy.16 = f32[128]{0:T(128)} copy(f32[128]{0:T(128)} %bitcast.1) | data formatting | bytes 1024
  105.1 1.9 %copy.17 = f32[128,1152]{1,0:T(8,128)} copy(f32[128,1152]{1,0:T(8,128)} %get-tuple-element.17) | data formatting | bytes 1179648
  107.0 1.9 %copy.18 = f32[128,1152]{1,0:T(8,128)} copy(f32[128,1152]{1,0:T(8,128)} %get-tuple-element.18) | data formatting | bytes 1179648
  108.9 1.3 %copy.19 = f32[9,288]{1,0:T(8,128)} copy(f32[9,288]{1,0:T(8,128)} %get-tuple-element.19) | data formatting | bytes 20736

commit v2 on v1

--- a/solution.py
+++ b/solution.py
@@ -1,5 +1,3 @@
-import functools
-
 import jax
 import jax.numpy as jnp
 import numpy as np
@@ -16,13 +14,16 @@
 D = 1152
 COLS = D // 4
 PIECE = 80
+PART = 64
+PARTS = ROWS // PART
 HALF = 8 * PIECE
 EPS = 1e-06
 BF = jnp.bfloat16
 F32 = jnp.float32
 
-R_RAW, R_SIB, R_LOSS, R_EMB, R_PRE, R_ONE, R_FIN, R_ALL = 12, 13, 14, 15, 18, 21, 35, 43
-S_K, S_RAW, S_Q, S_SIB, S_LOSS, S_EMB, S_PRE, S_ONE, S_FIN, S_ALL = 0, 10, 11, 12, 13, 14, 17, 20, 34, 50
+R_K, R_TEXT, R_RT, R_RI, R_RAW, R_SIB, R_LOSS, R_EMB, R_PRE = 0, 24, 36, 40, 48, 49, 50, 51, 54
+R_ONE, R_FIN, R_ALL = 57, 71, 79
+S_RAW, S_SIB, S_LOSS, S_EMB, S_PRE, S_ONE, S_FIN, S_RT, S_RI, S_K, S_ALL = 0, 1, 2, 3, 6, 9, 23, 39, 43, 51, 100
 
 
 def nt(left, right):
@@ -44,7 +45,7 @@
 def kernel(
     nem, bias, img, txt, w_any, sel_any,
     loss_o, ig_o, tg_o, hg_o,
-    w, sel, kbuf, raw, qf, unit, acc, pre, pre_t, sib_f32, sib_bf, loss_s, loss_r,
+    w, sel, kbuf, tbuf, rt, ri, raw, qf, unit, acc, pre, pre_t, sib_f32, sib_bf, loss_s, loss_r,
     emb_t, p_t, p_out, one, fin_s, fin_r, ssem, rsem, lsem,
 ):
     dp = lax.axis_index("dp")
@@ -66,6 +67,10 @@
     chain_to = (lax.rem(dp + 1 + 126 * core, 128), lax.rem(yh + flip_to, 2) * 2 + core)
     chain_from = (lax.rem(dp + 127 - 126 * core, 128), lax.rem(yh + flip_from, 2) * 2 + core)
 
+    column = (lax.rem(dp + jnp.where(z == 0, 7, 121), 128), pair)
+    row_up = (lax.rem(dp + 8, 128), lax.rem(yh + jnp.where(yl == 3, 1, 0), 2) * 2 + core)
+    row_down = (lax.rem(dp + 120, 128), lax.rem(yh + jnp.where(yl == 0, 1, 0), 2) * 2 + core)
+
     def x_dev(d):
         return chip(lax.rem(x + d, NX), y, z, core)
 
@@ -116,6 +121,21 @@
         hello(sibling)
         hello(across)
         hello(chain_from)
+        hello(chain_to)
+
+        @pl.when(z == 0)
+        def _():
+            hello(column)
+            hello(row_down)
+
+        if role == 1:
+
+            @pl.when(z == NZ - 1)
+            def _():
+                hello(column)
+                hello(row_up)
+
+        at_wrap = jnp.where(jnp.logical_or(z == 0, z == NZ - 1), 1 + role, 0)
         if role == 0:
             sel_copy = pltpu.make_async_copy(sel_any, sel, lsem.at[1])
             sel_copy.start()
@@ -129,69 +149,134 @@
             pl.when(jnp.logical_not(is_me(device)))(lambda device=device: hello(device))
 
         started = []
+        next_send = [S_K]
 
         def go(*args):
             c = copy(*args)
             c.start()
             started.append(c)
 
-        def kslot(t, h, s):
-            return kbuf.at[t, h, pl.ds(s * ROWS, ROWS)]
+        def move(src, dst, recv, device):
+            go(src, dst, next_send[0], recv, device)
+            next_send[0] += 1
+
+        def kslot(t, h, s, u):
+            return kbuf.at[t, h, pl.ds(s * ROWS + u * PART, PART)]
+
+        def k_sem(t, h, s, u):
+            return R_K + 8 * t + 4 * h + 2 * s + u
 
         def arrived(dst, recv):
             copy(dst, dst, 0, recv, sibling).wait_recv()
 
-        def spread(s, send):
-            go(kslot(0, 0, s), kslot(1, 0, s), send, 4 + s, chain_to)
-            go(kslot(0, 0, s), kslot(0, 1, s), send + 1, 2 + s, across)
+        text_to = chain_to if role == 0 else chain_from
+
+        def tslot(t, h, u):
+            return kslot(t, h, 0, u) if role == 0 else tbuf.at[t, h, pl.ds(u * PART, PART)]
+
+        def t_sem(t, h, u):
+            return R_TEXT + 4 * t + 2 * h + u
+
+        def chain(src, dst, recv, device, h, wrap, relay_dst, relay_recv):
+            if h == 1:
+                move(src, dst, recv, device)
+                return
+            direct = copy(src, dst, next_send[0], recv, device)
+            relayed = copy(src, relay_dst, next_send[0], relay_recv, column)
+            next_send[0] += 1
+            pl.when(z != wrap)(lambda: direct.start())
+            pl.when(z == wrap)(lambda: relayed.start())
+            started.append(direct)
+
+        def text_on(t, h, parts=range(PARTS)):
+            for u in parts:
+                if t or h:
+                    arrived(tslot(t, h, u), t_sem(t, h, u))
+                if t < WINDOW - 1:
+                    chain(
+                        tslot(t, h, u), tslot(t + 1, h, u), t_sem(t + 1, h, u), text_to, h,
+                        NZ - 1, rt.at[min(t, 1), pl.ds(u * PART, PART)], R_RT + 2 * t + u,
+                    )
+                if t == 0 and h == 0:
+                    move(tslot(0, 0, u), tslot(0, 1, u), t_sem(0, 1, u), across)
+                if role == 1:
+                    move(tslot(t, h, u), kslot(t, h, 1, u), k_sem(t, h, 1, u), sibling)
+
+        def image_on(t, h, parts=((1, 0), (1, 1), (0, 0), (0, 1))):
+            for s, u in parts:
+                if t or h or s == 0:
+                    arrived(kslot(t, h, s, u), k_sem(t, h, s, u))
+                if t < WINDOW - 1:
+                    chain(
+                        kslot(t, h, s, u), kslot(t + 1, h, s, u), k_sem(t + 1, h, s, u), chain_to, h,
+                        0, ri.at[min(t, 1), pl.ds(s * ROWS + u * PART, PART)],
+                        R_RI + 4 * t + 2 * s + u,
+                    )
+
+        later = []
+
+        def relay(src, dst, recv_in, send, recv_out, device, where):
+            c = copy(src, dst, send, recv_out, device)
+
+            @pl.when(z == where)
+            def _():
+                arrived(src, recv_in)
+                c.start()
+
+            later.append((c, where))
+
+        def relay_text(t):
+            for u in range(PARTS):
+                relay(
+                    rt.at[t, pl.ds(u * PART, PART)], tslot(t + 1, 0, u), R_RT + 2 * t + u,
+                    S_RT + 2 * t + u, t_sem(t + 1, 0, u), row_up, 0,
+                )
+
+        def relay_image(t):
+            for s, u in ((1, 0), (1, 1), (0, 0), (0, 1)):
+                i = 4 * t + 2 * s + u
+                relay(
+                    ri.at[t, pl.ds(s * ROWS + u * PART, PART)], kslot(t + 1, 0, s, u), R_RI + i,
+                    S_RI + i, k_sem(t + 1, 0, s, u), row_down, NZ - 1,
+                )
 
         t_unit, t_scale = normal(txt[...].astype(F32))
+        w_copy.wait()
+        i_unit, i_scale = normal(nn(img[...], w[...]))
         if role == 0:
             kbuf[0, 0, own_rows] = t_unit.astype(BF)
-            away = 3 + 3 + 14 + 16
+            unit[own_rows] = i_unit
+            qf[own_rows] = i_unit.astype(BF)
+            raw[own_rows] = img[...]
+            away = 4 + 3 + 14 + 16 + at_wrap
             for h in range(2):
                 for d in range(8):
                     away = away - jnp.where(is_me(fin_dev(h, d)), 1, 0)
             pl.semaphore_wait(barrier, away)
-            spread(own, S_K)
+            text_on(0, 0)
+            for u in range(PARTS):
+                move(qf.at[pl.ds(u * PART, PART)], kslot(0, 0, 0, u), k_sem(0, 0, 0, u), sibling)
             go(txt, raw.at[own_rows], S_RAW, R_RAW, sibling)
-            w_copy.wait()
-            i_unit, i_scale = normal(nn(img[...], w[...]))
-            unit[own_rows] = i_unit
-            qf[own_rows] = i_unit.astype(BF)
-            go(qf.at[own_rows], kslot(0, 0, own), S_Q, own, sibling)
-            raw[own_rows] = img[...]
+            arrived(raw.at[oth_rows], R_RAW)
+            o_unit, oth_scale = normal(nn(raw[oth_rows], w[...]))
         else:
+            tbuf[0, 0] = t_unit.astype(BF)
             unit[own_rows] = t_unit
             qf[own_rows] = t_unit.astype(BF)
-            pl.semaphore_wait(barrier, 3)
-            go(qf.at[own_rows], kslot(0, 0, own), S_Q, own, sibling)
+            kbuf[0, 0, own_rows] = i_unit.astype(BF)
+            raw[own_rows] = txt[...]
+            pl.semaphore_wait(barrier, 4 + at_wrap)
+            text_on(0, 0)
             go(img, raw.at[own_rows], S_RAW, R_RAW, sibling)
-            w_copy.wait()
-            i_unit, i_scale = normal(nn(img[...], w[...]))
-            kbuf[0, 0, own_rows] = i_unit.astype(BF)
-            spread(own, S_K)
-            raw[own_rows] = txt[...]
+            image_on(0, 0)
+            arrived(raw.at[oth_rows], R_RAW)
+            o_unit, oth_scale = normal(raw[oth_rows].astype(F32))
         own_scale = i_scale if role == 0 else t_scale
-        arrived(kslot(0, 0, oth), oth)
-        spread(oth, S_K + 2)
-        arrived(raw.at[oth_rows], R_RAW)
-        if role == 0:
-            o_unit, oth_scale = normal(nn(raw[oth_rows], w[...]))
-        else:
-            o_unit, oth_scale = normal(raw[oth_rows].astype(F32))
         unit[oth_rows] = o_unit
         qf[oth_rows] = o_unit.astype(BF)
 
         gain = jnp.exp(jnp.full((1, 1), nem[0], F32))
         shift = bias[0]
-        if role == 0:
-            sel_copy.wait()
-            for part in range(4):
-                rows = pl.ds(part * (HALF // 2), HALF // 2)
-                emb_t[0, rows] = nt(sel[rows], raw[...]).astype(BF)
-            for d in range(1, NX):
-                go(emb_t.at[0], emb_t.at[d], S_EMB + d - 1, R_EMB + d - 1, x_dev(d))
 
         loss = jnp.zeros((BLOCK, 1), F32)
 
@@ -218,18 +303,65 @@
                 acc[...] += value
             return loss
 
-        loss = score(0, 0, loss)
-        send = S_K + 4
-        for t, h in ((1, 0), (0, 1), (1, 1)):
-            for s in (own, oth):
-                arrived(kslot(t, h, s), 4 * t + 2 * h + s)
-                go(kslot(t, h, s), kslot(t + 1, h, s), send, 4 * t + 4 + 2 * h + s, chain_to)
-                send += 1
-            loss = score(t, h, loss)
-        for h in range(2):
-            for s in (own, oth):
-                arrived(kslot(2, h, s), 8 + 2 * h + s)
-            loss = score(2, h, loss)
+        if role == 0:
+
+            def ready(t, h):
+                for u in range(PARTS):
+                    arrived(kslot(t, h, 1, u), k_sem(t, h, 1, u))
+
+            ready(0, 0)
+            loss = score(0, 0, loss)
+            sel_copy.wait()
+            for part in range(4):
+                rows = pl.ds(part * (HALF // 2), HALF // 2)
+                emb_t[0, rows] = nt(sel[rows], raw[...]).astype(BF)
+            for d in range(1, NX):
+                go(emb_t.at[0], emb_t.at[d], S_EMB + d - 1, R_EMB + d - 1, x_dev(d))
+            relay_text(0)
+            text_on(1, 0)
+            text_on(0, 1)
+            relay_text(1)
+            ready(1, 0)
+            loss = score(1, 0, loss)
+            text_on(1, 1)
+            ready(0, 1)
+            loss = score(0, 1, loss)
+            text_on(2, 0)
+            ready(2, 0)
+            loss = score(2, 0, loss)
+            ready(1, 1)
+            loss = score(1, 1, loss)
+            text_on(2, 1)
+            ready(2, 1)
+            loss = score(2, 1, loss)
+        else:
+            relay_text(0)
+            relay_image(0)
+            text_on(1, 0)
+            image_on(1, 0)
+            text_on(0, 1, (0,))
+            for s in (1, 0):
+                for u in range(PARTS):
+                    move(kslot(0, 0, s, u), kslot(0, 1, s, u), k_sem(0, 1, s, u), across)
+            text_on(0, 1, (1,))
+            relay_text(1)
+            text_on(1, 1)
+            text_on(2, 0)
+            relay_image(1)
+            loss = score(0, 0, loss)
+            text_on(2, 1)
+            loss = score(1, 0, loss)
+            order = ((1, 0), (1, 1), (0, 0), (0, 1))
+            image_on(0, 1, order[:2])
+            for i in range(2):
+                image_on(1, 1, order[i : i + 1])
+                image_on(0, 1, order[i + 2 : i + 3])
+            loss = score(0, 1, loss)
+            image_on(1, 1, order[2:])
+            loss = score(1, 1, loss)
+            for h in range(2):
+                image_on(2, h)
+                loss = score(2, h, loss)
 
         for half_rows, scale in ((own_rows, own_scale), (oth_rows, oth_scale)):
             u = unit[half_rows]
@@ -324,6 +456,8 @@
         hg_o[...] = total[0:9]
         for c in started:
             c.wait_send()
+        for c, where in later:
+            pl.when(z == where)(lambda c=c: c.wait_send())
         if role == 0:
             for h in range(2):
                 for d in range(8):
@@ -335,6 +469,13 @@
 
     pl.when(core == 0)(lambda: run(0))
     pl.when(core == 1)(lambda: run(1))
+
+
+def results(loss, ig, tg, hg, loss_o, ig_o, tg_o, hg_o):
+    loss_o[...] = loss[0, :]
+    ig_o[...] = ig[...]
+    tg_o[...] = tg[...]
+    hg_o[...] = hg[...]
 
 
 def body(image_emb, text_emb, head_weight, natural_exponent_multiplier, bias):
@@ -356,6 +497,9 @@
             pltpu.VMEM((D, D), BF),
             pltpu.VMEM((2 * HALF, D), BF),
             pltpu.VMEM((WINDOW, 2, BLOCK, D), BF),
+            pltpu.VMEM((WINDOW, 2, ROWS, D), BF),
+            pltpu.VMEM((2, ROWS, D), BF),
+            pltpu.VMEM((2, BLOCK, D), BF),
             pltpu.VMEM((BLOCK, D), BF),
             pltpu.VMEM((BLOCK, D), BF),
             pltpu.VMEM((BLOCK, D), F32),
@@ -387,7 +531,20 @@
         head_weight,
         jnp.asarray(select_matrix(), BF),
     )
-    return loss.reshape(ROWS), image_grad, text_grad, head_grad
+    return tuple(
+        pl.pallas_call(
+            results,
+            name="results",
+            out_shape=(
+                jax.ShapeDtypeStruct((ROWS,), F32),
+                jax.ShapeDtypeStruct((ROWS, D), F32),
+                jax.ShapeDtypeStruct((ROWS, D), F32),
+                jax.ShapeDtypeStruct((9, COLS), F32),
+            ),
+            in_specs=[vmem] * 4,
+            out_specs=(vmem,) * 4,
+        )(loss, image_grad, text_grad, head_grad)
+    )
 
 
 def solution(mesh):

time: 111 us -> 100 us (0.901)
  the two profiles are of different devices: /device:TPU:12 before, /device:TPU:56 now
where the time goes in v2:
time: 100 us; the launch traced here: 98.5 us
  Pallas kernels  96.6 us (97%)
  between operations  1.93 us (2%)
    pallas_call x1, Pallas kernels, body(): pl.pallas_call(kernel, name='contrast', out_shape=(jax.ShapeDtypeStruct((...  94.3 us
    pallas_call x1, Pallas kernels, body(): pl.pallas_call(results, name='results', out_shape=(jax.ShapeDtypeStruct((...  2.31 us

profile of v2, /device:TPU:56, one launch (start us, length us, event | category | flops | bytes accessed | tf_op | source)
XLA Modules:
  0.0 98.5 jit_solution(2967845950797556159)
XLA Ops:
  1.9 94.3 %contrast.1 = (f32[1,128]{1,0:T(1,128)}, f32[128,1152]{1,0:T(8,128)}, f32[128,1152]{1,0:T(8,128)}, f32[9,288]{1,0:T(8,128)}) custom-call(f32[1]{0:T(128)S(6)} %copy.10.nem, f32[1]{0:T(128)S(6)} %copy.11.bias, bf16[128,1152]{1,0:T(8,128)(2,1)} %img.1, bf16[128,1152]{1,0:T(8,128)(2,1)} %txt.1, bf16[1152,1152]{1,0:T(8,128)(2,1)} %w_any.1, ...), custom_call_target="tpu_custom_call" | custom-call | tf_op jit(solution)/shard_map/contrast/pallas_call | solution.py:485
  96.2 2.3 %results.1 = (f32[128]{0:T(128)}, f32[128,1152]{1,0:T(8,128)}, f32[128,1152]{1,0:T(8,128)}, f32[9,288]{1,0:T(8,128)}) custom-call(f32[1,128]{1,0:T(1,128)} %get-tuple-element.8.loss, f32[128,1152]{1,0:T(8,128)} %get-tuple-element.9.ig, f32[128,1152]{1,0:T(8,128)} %get-tuple-element.10.tg, f32[9,288]{1,0:T(8,128)} %get-tuple-element.11.hg), custom_call_target="tpu_custom_call" | custom-call | tf_op jit(solution)/shard_map/results/pallas_call | solution.py:535

commit v3 on v2

--- a/solution.py
+++ b/solution.py
@@ -16,14 +16,21 @@
 PIECE = 80
 PART = 64
 PARTS = ROWS // PART
+BOTH = tuple((s, u) for s in (1, 0) for u in range(PARTS))
 HALF = 8 * PIECE
 EPS = 1e-06
 BF = jnp.bfloat16
 F32 = jnp.float32
 
-R_K, R_TEXT, R_RT, R_RI, R_RAW, R_SIB, R_LOSS, R_EMB, R_PRE = 0, 24, 36, 40, 48, 49, 50, 51, 54
-R_ONE, R_FIN, R_ALL = 57, 71, 79
-S_RAW, S_SIB, S_LOSS, S_EMB, S_PRE, S_ONE, S_FIN, S_RT, S_RI, S_K, S_ALL = 0, 1, 2, 3, 6, 9, 23, 39, 43, 51, 100
+R_RAW, R_SIB, R_LOSS, R_EMB, R_PRE, R_ONE, R_FIN, R_K = 0, 1, 2, 3, 6, 12, 26, 34
+R_TEXT = R_K + 12 * PARTS
+R_RT = R_TEXT + 6 * PARTS
+R_RI = R_RT + 2 * PARTS
+R_ALL = R_RI + 4 * PARTS
+S_RAW, S_SIB, S_LOSS, S_EMB, S_PRE, S_ONE, S_FIN, S_RT = 0, 1, 2, 3, 6, 12, 26, 42
+S_RI = S_RT + 2 * PARTS
+S_K = S_RI + 4 * PARTS
+S_ALL = S_K + 24 * PARTS
 
 
 def nt(left, right):
@@ -46,7 +53,7 @@
     nem, bias, img, txt, w_any, sel_any,
     loss_o, ig_o, tg_o, hg_o,
     w, sel, kbuf, tbuf, rt, ri, raw, qf, unit, acc, pre, pre_t, sib_f32, sib_bf, loss_s, loss_r,
-    emb_t, p_t, p_out, one, fin_s, fin_r, ssem, rsem, lsem,
+    emb_t, p_t, p_out, p_f32, one, fin_s, fin_r, ssem, rsem, lsem,
 ):
     dp = lax.axis_index("dp")
     pair = lax.axis_index("pair")
@@ -135,6 +142,10 @@
                 hello(column)
                 hello(row_up)
 
+        if role == 0:
+            hello((chain_from[0], chain_from[1] + 1))
+            pl.when(z == 0)(lambda: hello((row_down[0], row_down[1] + 1)))
+
         at_wrap = jnp.where(jnp.logical_or(z == 0, z == NZ - 1), 1 + role, 0)
         if role == 0:
             sel_copy = pltpu.make_async_copy(sel_any, sel, lsem.at[1])
@@ -164,7 +175,7 @@
             return kbuf.at[t, h, pl.ds(s * ROWS + u * PART, PART)]
 
         def k_sem(t, h, s, u):
-            return R_K + 8 * t + 4 * h + 2 * s + u
+            return R_K + (4 * t + 2 * h + s) * PARTS + u
 
         def arrived(dst, recv):
             copy(dst, dst, 0, recv, sibling).wait_recv()
@@ -175,7 +186,12 @@
             return kslot(t, h, 0, u) if role == 0 else tbuf.at[t, h, pl.ds(u * PART, PART)]
 
         def t_sem(t, h, u):
-            return R_TEXT + 4 * t + 2 * h + u
+            return R_TEXT + (2 * t + h) * PARTS + u
+
+        def text_next(t, h, u):
+            if role == 1 and t == 1:
+                return kslot(2, h, 1, u), k_sem(2, h, 1, u), (text_to[0], text_to[1] - 1)
+            return tslot(t + 1, h, u), t_sem(t + 1, h, u), text_to
 
         def chain(src, dst, recv, device, h, wrap, relay_dst, relay_recv):
             if h == 1:
@@ -193,16 +209,17 @@
                 if t or h:
                     arrived(tslot(t, h, u), t_sem(t, h, u))
                 if t < WINDOW - 1:
+                    dst, recv, device = text_next(t, h, u)
                     chain(
-                        tslot(t, h, u), tslot(t + 1, h, u), t_sem(t + 1, h, u), text_to, h,
-                        NZ - 1, rt.at[min(t, 1), pl.ds(u * PART, PART)], R_RT + 2 * t + u,
+                        tslot(t, h, u), dst, recv, device, h,
+                        NZ - 1, rt.at[t, pl.ds(u * PART, PART)], R_RT + PARTS * t + u,
                     )
                 if t == 0 and h == 0:
                     move(tslot(0, 0, u), tslot(0, 1, u), t_sem(0, 1, u), across)
                 if role == 1:
                     move(tslot(t, h, u), kslot(t, h, 1, u), k_sem(t, h, 1, u), sibling)
 
-        def image_on(t, h, parts=((1, 0), (1, 1), (0, 0), (0, 1))):
+        def image_on(t, h, parts=BOTH):
             for s, u in parts:
                 if t or h or s == 0:
                     arrived(kslot(t, h, s, u), k_sem(t, h, s, u))
@@ -210,7 +227,7 @@
                     chain(
                         kslot(t, h, s, u), kslot(t + 1, h, s, u), k_sem(t + 1, h, s, u), chain_to, h,
                         0, ri.at[min(t, 1), pl.ds(s * ROWS + u * PART, PART)],
-                        R_RI + 4 * t + 2 * s + u,
+                        R_RI + (2 * t + s) * PARTS + u,
                     )
 
         later = []
@@ -227,14 +244,16 @@
 
         def relay_text(t):
             for u in range(PARTS):
+                dst, recv, device = text_next(t, 0, u)
+                device = (row_up[0], row_up[1] - 1) if device is not text_to else row_up
                 relay(
-                    rt.at[t, pl.ds(u * PART, PART)], tslot(t + 1, 0, u), R_RT + 2 * t + u,
-                    S_RT + 2 * t + u, t_sem(t + 1, 0, u), row_up, 0,
+                    rt.at[t, pl.ds(u * PART, PART)], dst, R_RT + PARTS * t + u,
+                    S_RT + PARTS * t + u, recv, device, 0,
                 )
 
         def relay_image(t):
-            for s, u in ((1, 0), (1, 1), (0, 0), (0, 1)):
-                i = 4 * t + 2 * s + u
+            for s, u in BOTH:
+                i = (2 * t + s) * PARTS + u
                 relay(
                     ri.at[t, pl.ds(s * ROWS + u * PART, PART)], kslot(t + 1, 0, s, u), R_RI + i,
                     S_RI + i, k_sem(t + 1, 0, s, u), row_down, NZ - 1,
@@ -265,7 +284,7 @@
             qf[own_rows] = t_unit.astype(BF)
             kbuf[0, 0, own_rows] = i_unit.astype(BF)
             raw[own_rows] = txt[...]
-            pl.semaphore_wait(barrier, 4 + at_wrap)
+            pl.semaphore_wait(barrier, 5 + at_wrap + jnp.where(z == 0, 1, 0))
             text_on(0, 0)
             go(img, raw.at[own_rows], S_RAW, R_RAW, sibling)
             image_on(0, 0)
@@ -319,8 +338,8 @@
                 go(emb_t.at[0], emb_t.at[d], S_EMB + d - 1, R_EMB + d - 1, x_dev(d))
             relay_text(0)
             text_on(1, 0)
+            relay_text(1)
             text_on(0, 1)
-            relay_text(1)
             ready(1, 0)
             loss = score(1, 0, loss)
             text_on(1, 1)
@@ -339,25 +358,21 @@
             relay_image(0)
             text_on(1, 0)
             image_on(1, 0)
-            text_on(0, 1, (0,))
-            for s in (1, 0):
-                for u in range(PARTS):
-                    move(kslot(0, 0, s, u), kslot(0, 1, s, u), k_sem(0, 1, s, u), across)
-            text_on(0, 1, (1,))
             relay_text(1)
-            text_on(1, 1)
-            text_on(2, 0)
+            text_on(0, 1, range(PARTS // 2))
+            for s, u in BOTH:
+                move(kslot(0, 0, s, u), kslot(0, 1, s, u), k_sem(0, 1, s, u), across)
+            text_on(0, 1, range(PARTS // 2, PARTS))
             relay_image(1)
             loss = score(0, 0, loss)
-            text_on(2, 1)
+            text_on(1, 1)
             loss = score(1, 0, loss)
-            order = ((1, 0), (1, 1), (0, 0), (0, 1))
-            image_on(0, 1, order[:2])
-            for i in range(2):
-                image_on(1, 1, order[i : i + 1])
-                image_on(0, 1, order[i + 2 : i + 3])
+            image_on(0, 1, BOTH[:2])
+            for i in range(2 * PARTS - 2):
+                image_on(1, 1, BOTH[i : i + 1])
+                image_on(0, 1, BOTH[i + 2 : i + 3])
             loss = score(0, 1, loss)
-            image_on(1, 1, order[2:])
+            image_on(1, 1, BOTH[2 * PARTS - 2 :])
             loss = score(1, 1, loss)
             for h in range(2):
                 image_on(2, h)
@@ -371,15 +386,19 @@
             if role == 0:
                 pre[half_rows] = g.astype(BF)
                 pre_t[:, half_rows] = jnp.transpose(g).astype(BF)
+                part = 0 if half_rows is own_rows else 1
+                for d in range(1, NX):
+                    start = pl.multiple_of(lax.rem(x + d, NX) * COLS, 16)
+                    go(
+                        pre_t.at[pl.ds(start, COLS), half_rows], p_t.at[d, :, half_rows],
+                        S_PRE + 2 * d - 2 + part, R_PRE + 2 * d - 2 + part, x_dev(d),
+                    )
             elif half_rows is own_rows:
                 tg_o[...] = g
             else:
                 unit[half_rows] = g
 
         if role == 0:
-            for d in range(1, NX):
-                start = pl.multiple_of(lax.rem(x + d, NX) * COLS, 16)
-                go(pre_t.at[pl.ds(start, COLS)], p_t.at[d], S_PRE + d - 1, R_PRE + d - 1, x_dev(d))
             go(pre.at[oth_rows], sib_bf, S_SIB, R_SIB, sibling)
             turned = jnp.transpose(jnp.broadcast_to(loss, (BLOCK, 128)))
             loss_o[...] = turned[0:1, 0:ROWS]
@@ -388,23 +407,28 @@
             start = pl.multiple_of(x * COLS, 16)
             p_t[0] = pre_t[pl.ds(start, COLS)]
             for d in range(1, NX):
-                arrived(p_t.at[d], R_PRE + d - 1)
+                for part in range(2):
+                    arrived(p_t.at[d, :, pl.ds(part * ROWS, ROWS)], R_PRE + 2 * d - 2 + part)
                 arrived(emb_t.at[d], R_EMB + d - 1)
 
-            def product(h, d):
+            def piece(h, d):
                 index = lax.rem((y if h == 0 else z) + d, 8)
-                rows = pl.ds(pl.multiple_of(h * HALF + index * PIECE, 16), PIECE)
-                total = nt(emb_t[0, rows], p_t[0])
-                for k in range(1, NX):
-                    total = total + nt(emb_t[k, rows], p_t[k])
-                return total
-
-            for d in (4, 3, 5, 2, 6, 1, 7):
-                for h in range(2):
+                return pl.ds(pl.multiple_of(h * HALF + index * PIECE, 16), PIECE)
+
+            totals = []
+            for h in range(2):
+                for tile in range(2):
+                    rows = pl.ds(h * HALF + tile * (HALF // 2), HALF // 2)
+                    total = nt(emb_t[0, rows], p_t[0])
+                    for k in range(1, NX):
+                        total = total + nt(emb_t[k, rows], p_t[k])
+                    p_f32[rows] = total
+                    p_out[rows] = total.astype(BF)
+                for d in (4, 3, 5, 2, 6, 1, 7):
                     i = 7 * h + d - 1
-                    p_out[i] = product(h, d).astype(BF)
-                    go(p_out.at[i], one.at[i], S_ONE + i, R_ONE + i, one_dev(h, d))
-            totals = [product(0, 0), product(1, 0)]
+                    go(p_out.at[piece(h, d)], one.at[i], S_ONE + i, R_ONE + i, one_dev(h, d))
+            for h in range(2):
+                totals.append(p_f32[piece(h, 0)])
             ig_o[...] = nt(pre[own_rows], w[...])
             r = lax.broadcasted_iota(jnp.int32, (128, PIECE), 0)
             c = lax.broadcasted_iota(jnp.int32, (128, PIECE), 1)
@@ -512,7 +536,8 @@
             pltpu.VMEM((8, ROWS), F32),
             pltpu.VMEM((NX, 2 * HALF, BLOCK), BF),
             pltpu.VMEM((NX, COLS, BLOCK), BF),
-            pltpu.VMEM((14, PIECE, COLS), BF),
+            pltpu.VMEM((2 * HALF, COLS), BF),
+            pltpu.VMEM((2 * HALF, COLS), F32),
             pltpu.VMEM((14, PIECE, COLS), BF),
             pltpu.VMEM((2, 8, 16, COLS), BF),
             pltpu.VMEM((8, 16, COLS), BF),

time: 100 us -> 96.7 us (0.967)
  the two profiles are of different devices: /device:TPU:56 before, /device:TPU:22 now
where the time goes in v3:
time: 96.7 us; the launch traced here: 96.5 us
  Pallas kernels  94.6 us (98%)
  between operations  1.93 us (2%)
    pallas_call x1, Pallas kernels, body(): pl.pallas_call(kernel, name='contrast', out_shape=(jax.ShapeDtypeStruct((...  92.3 us
    pallas_call x1, Pallas kernels, body(): pl.pallas_call(results, name='results', out_shape=(jax.ShapeDtypeStruct((...  2.31 us

profile of v3, /device:TPU:22, one launch (start us, length us, event | category | flops | bytes accessed | tf_op | source)
XLA Modules:
  0.0 96.5 jit_solution(10856833574537676149)
XLA Ops:
  1.9 92.3 %contrast.1 = (f32[1,128]{1,0:T(1,128)}, f32[128,1152]{1,0:T(8,128)}, f32[128,1152]{1,0:T(8,128)}, f32[9,288]{1,0:T(8,128)}) custom-call(f32[1]{0:T(128)S(6)} %copy.10.nem, f32[1]{0:T(128)S(6)} %copy.11.bias, bf16[128,1152]{1,0:T(8,128)(2,1)} %img.1, bf16[128,1152]{1,0:T(8,128)(2,1)} %txt.1, bf16[1152,1152]{1,0:T(8,128)(2,1)} %w_any.1, ...), custom_call_target="tpu_custom_call" | custom-call | tf_op jit(solution)/shard_map/contrast/pallas_call | solution.py:509
  94.2 2.3 %results.1 = (f32[128]{0:T(128)}, f32[128,1152]{1,0:T(8,128)}, f32[128,1152]{1,0:T(8,128)}, f32[9,288]{1,0:T(8,128)}) custom-call(f32[1,128]{1,0:T(1,128)} %get-tuple-element.8.loss, f32[128,1152]{1,0:T(8,128)} %get-tuple-element.9.ig, f32[128,1152]{1,0:T(8,128)} %get-tuple-element.10.tg, f32[9,288]{1,0:T(8,128)} %get-tuple-element.11.hg), custom_call_target="tpu_custom_call" | custom-call | tf_op jit(solution)/shard_map/results/pallas_call | solution.py:560

commit v4 on v3

--- a/solution.py
+++ b/solution.py
@@ -357,12 +357,12 @@
             relay_text(0)
             relay_image(0)
             text_on(1, 0)
-            image_on(1, 0)
             relay_text(1)
             text_on(0, 1, range(PARTS // 2))
             for s, u in BOTH:
                 move(kslot(0, 0, s, u), kslot(0, 1, s, u), k_sem(0, 1, s, u), across)
             text_on(0, 1, range(PARTS // 2, PARTS))
+            image_on(1, 0)
             relay_image(1)
             loss = score(0, 0, loss)
             text_on(1, 1)

time: 96.7 us -> 91.3 us (0.944)
  the two profiles are of different devices: /device:TPU:22 before, /device:TPU:56 now
where the time goes in v4:
time: 91.3 us; the launch traced here: 91.1 us
  Pallas kernels  89.2 us (98%)
  between operations  1.93 us (2%)
    pallas_call x1, Pallas kernels, body(): pl.pallas_call(kernel, name='contrast', out_shape=(jax.ShapeDtypeStruct((...  86.9 us
    pallas_call x1, Pallas kernels, body(): pl.pallas_call(results, name='results', out_shape=(jax.ShapeDtypeStruct((...  2.31 us

profile of v4, /device:TPU:56, one launch (start us, length us, event | category | flops | bytes accessed | tf_op | source)
XLA Modules:
  0.0 91.1 jit_solution(9510255873453159849)
XLA Ops:
  1.9 86.9 %contrast.1 = (f32[1,128]{1,0:T(1,128)}, f32[128,1152]{1,0:T(8,128)}, f32[128,1152]{1,0:T(8,128)}, f32[9,288]{1,0:T(8,128)}) custom-call(f32[1]{0:T(128)S(6)} %copy.10.nem, f32[1]{0:T(128)S(6)} %copy.11.bias, bf16[128,1152]{1,0:T(8,128)(2,1)} %img.1, bf16[128,1152]{1,0:T(8,128)(2,1)} %txt.1, bf16[1152,1152]{1,0:T(8,128)(2,1)} %w_any.1, ...), custom_call_target="tpu_custom_call" | custom-call | tf_op jit(solution)/shard_map/contrast/pallas_call | solution.py:509
  88.8 2.3 %results.1 = (f32[128]{0:T(128)}, f32[128,1152]{1,0:T(8,128)}, f32[128,1152]{1,0:T(8,128)}, f32[9,288]{1,0:T(8,128)}) custom-call(f32[1,128]{1,0:T(1,128)} %get-tuple-element.8.loss, f32[128,1152]{1,0:T(8,128)} %get-tuple-element.9.ig, f32[128,1152]{1,0:T(8,128)} %get-tuple-element.10.tg, f32[9,288]{1,0:T(8,128)} %get-tuple-element.11.hg), custom_call_target="tpu_custom_call" | custom-call | tf_op jit(solution)/shard_map/results/pallas_call | solution.py:560

commit v5 on v4

--- a/solution.py
+++ b/solution.py
@@ -364,13 +364,13 @@
             text_on(0, 1, range(PARTS // 2, PARTS))
             image_on(1, 0)
             relay_image(1)
+            text_on(1, 1)
             loss = score(0, 0, loss)
-            text_on(1, 1)
-            loss = score(1, 0, loss)
             image_on(0, 1, BOTH[:2])
             for i in range(2 * PARTS - 2):
                 image_on(1, 1, BOTH[i : i + 1])
                 image_on(0, 1, BOTH[i + 2 : i + 3])
+            loss = score(1, 0, loss)
             loss = score(0, 1, loss)
             image_on(1, 1, BOTH[2 * PARTS - 2 :])
             loss = score(1, 1, loss)

time: 91.3 us -> 91.2 us (level)
  no operation moved by 1% of the time
where the time goes in v5:
time: 91.2 us; the launch traced here: 90.3 us
  Pallas kernels  88.4 us (97%)
  between operations  1.93 us (2%)
    pallas_call x1, Pallas kernels, body(): pl.pallas_call(kernel, name='contrast', out_shape=(jax.ShapeDtypeStruct((...  86.1 us
    pallas_call x1, Pallas kernels, body(): pl.pallas_call(results, name='results', out_shape=(jax.ShapeDtypeStruct((...  2.31 us

profile of v5, /device:TPU:56, one launch (start us, length us, event | category | flops | bytes accessed | tf_op | source)
XLA Modules:
  0.0 90.3 jit_solution(137633943029409662)
XLA Ops:
  1.9 86.1 %contrast.1 = (f32[1,128]{1,0:T(1,128)}, f32[128,1152]{1,0:T(8,128)}, f32[128,1152]{1,0:T(8,128)}, f32[9,288]{1,0:T(8,128)}) custom-call(f32[1]{0:T(128)S(6)} %copy.10.nem, f32[1]{0:T(128)S(6)} %copy.11.bias, bf16[128,1152]{1,0:T(8,128)(2,1)} %img.1, bf16[128,1152]{1,0:T(8,128)(2,1)} %txt.1, bf16[1152,1152]{1,0:T(8,128)(2,1)} %w_any.1, ...), custom_call_target="tpu_custom_call" | custom-call | tf_op jit(solution)/shard_map/contrast/pallas_call | solution.py:509
  88.0 2.3 %results.1 = (f32[128]{0:T(128)}, f32[128,1152]{1,0:T(8,128)}, f32[128,1152]{1,0:T(8,128)}, f32[9,288]{1,0:T(8,128)}) custom-call(f32[1,128]{1,0:T(1,128)} %get-tuple-element.8.loss, f32[128,1152]{1,0:T(8,128)} %get-tuple-element.9.ig, f32[128,1152]{1,0:T(8,128)} %get-tuple-element.10.tg, f32[9,288]{1,0:T(8,128)} %get-tuple-element.11.hg), custom_call_target="tpu_custom_call" | custom-call | tf_op jit(solution)/shard_map/results/pallas_call | solution.py:560
